TPU v7x, 32 devices: a whole 2x2x4 slice. The times are simulated.
32 devices in a mesh: ctx: 4 (over y, x), ch: 8 (over z, core).
Axes of the slice: x: 2, y: 2, z: 4, core: 2. Of those that a mesh axis runs over, the one named last changes fastest.
Arguments:
- queries: bfloat16 [4096, 4096], P('ctx', 'ch'), may hold values from -12 to 12
- key_input: bfloat16 [4096, 4096], P('ctx', 'ch'), may hold values from -6 to 6
- value_input: bfloat16 [4096, 4096], P('ctx', 'ch'), may hold values from -6 to 6
- filters: bfloat16 [4096, 4096], P('ctx', 'ch'), may hold values from -0.3 to 0.3
- skip_gain: float32 [4096], P('ch'), may hold values from -0.3 to 0.3
- out_weight: bfloat16 [4096, 4096], P('ch'), may hold values from -0.125 to 0.125
Outputs:
- layer_out: bfloat16 [4096, 4096], P('ctx', 'ch')
All inputs are finite; a program needn't handle non-finite values.
Results may differ from a plain program's by a relative error of at most 0.019.
Values may be sent and summed in bfloat16 or wider, within the bound.
A program may use at most 320 MiB of HBM per device.

v0:
```python
import jax
import jax.numpy as jnp
from jax import lax
from jax.sharding import PartitionSpec as P

outer_radix = 64


def shifted(block, axis, distance):
    devices = range(lax.axis_size(axis))
    route = [(i - distance, i) for i in devices if i - distance in devices]
    return lax.ppermute(block, axis, route)


def split_pieces(values):
    if values.dtype == jnp.bfloat16:
        return [(values, 0)]
    high_part = values.astype(jnp.bfloat16)
    low_part = (values - high_part.astype(jnp.float32)).astype(jnp.bfloat16)
    return [(high_part, 0), (low_part, 1)]


def split_dot(form, left, right):
    total = None
    for left_piece, left_order in split_pieces(left):
        for right_piece, right_order in split_pieces(right):
            if left_order + right_order <= 1:
                term = jnp.einsum(form, left_piece, right_piece, preferred_element_type=jnp.float32)
                total = term if total is None else total + term
    return total


def angle_table(rows, columns, period):
    row_index = jnp.arange(rows, dtype=jnp.int32)[:, None]
    col_index = jnp.arange(columns, dtype=jnp.int32)[None, :]
    phases = row_index * col_index % period
    angles = phases.astype(jnp.float32) * (2.0 * jnp.pi / period)
    return (jnp.cos(angles), jnp.sin(angles))


def forward(signal, length):
    inner_len = length // outer_radix
    used_rows = signal.shape[0] // inner_len
    columns = signal.shape[1]
    folded = signal.reshape(used_rows, inner_len, columns)
    cos_outer, sin_outer = angle_table(outer_radix, used_rows, outer_radix)
    first_real = split_dot("kn,nqc->kqc", cos_outer, folded)
    first_imag = -split_dot("kn,nqc->kqc", sin_outer, folded)
    cos_twist, sin_twist = angle_table(outer_radix, inner_len, length)
    cos_twist = cos_twist[:, :, None]
    sin_twist = sin_twist[:, :, None]
    twist_real = first_real * cos_twist + first_imag * sin_twist
    twist_imag = first_imag * cos_twist - first_real * sin_twist
    cos_inner, sin_inner = angle_table(inner_len, inner_len, inner_len)
    spec_real = split_dot("kqc,qm->kmc", twist_real, cos_inner) + split_dot(
        "kqc,qm->kmc", twist_imag, sin_inner
    )
    spec_imag = split_dot("kqc,qm->kmc", twist_imag, cos_inner) - split_dot(
        "kqc,qm->kmc", twist_real, sin_inner
    )
    return (spec_real, spec_imag)


def inverse_tail(spec_real, spec_imag, length):
    inner_len = length // outer_radix
    cos_inner, sin_inner = angle_table(inner_len, inner_len, inner_len)
    back_real = split_dot("kmc,mq->kqc", spec_real, cos_inner) - split_dot(
        "kmc,mq->kqc", spec_imag, sin_inner
    )
    back_imag = split_dot("kmc,mq->kqc", spec_imag, cos_inner) + split_dot(
        "kmc,mq->kqc", spec_real, sin_inner
    )
    cos_twist, sin_twist = angle_table(outer_radix, inner_len, length)
    cos_twist = cos_twist[:, :, None]
    sin_twist = sin_twist[:, :, None]
    turn_real = back_real * cos_twist - back_imag * sin_twist
    turn_imag = back_imag * cos_twist + back_real * sin_twist
    cos_outer, sin_outer = angle_table(outer_radix, outer_radix, outer_radix)
    half_rows = outer_radix // 2
    tail_rows = split_dot("nk,kqc->nqc", cos_outer[half_rows:], turn_real) - split_dot(
        "nk,kqc->nqc", sin_outer[half_rows:], turn_imag
    )
    return tail_rows.reshape(half_rows * inner_len, -1) / length


def cycle_conv(mixed_in, filters, length):
    tok_rows, channels = mixed_in.shape
    all_segments = lax.all_gather(filters, "ctx", axis=0, tiled=True)
    padded = jnp.concatenate(
        [jnp.zeros((tok_rows, channels), all_segments.dtype), all_segments], axis=0
    )

    def add_lag(lag_index, held_block, sum_real, sum_imag):
        window = lax.dynamic_slice_in_dim(padded, lag_index * tok_rows, length, 0)
        filter_real, filter_imag = forward(window, length)
        input_real, input_imag = forward(held_block, length)
        sum_real = sum_real + input_real * filter_real - input_imag * filter_imag
        sum_imag = sum_imag + input_real * filter_imag + input_imag * filter_real
        return (sum_real, sum_imag)

    ctx_count = lax.axis_size("ctx")
    empty_spec = jnp.zeros((outer_radix, length // outer_radix, channels), jnp.float32)

    def cycle_step(lag_index, cycle_state):
        held_block, sum_real, sum_imag = cycle_state
        sum_real, sum_imag = add_lag(lag_index, held_block, sum_real, sum_imag)
        held_block = shifted(held_block, "ctx", 1)
        return (held_block, sum_real, sum_imag)

    held_block, sum_real, sum_imag = lax.fori_loop(
        0, ctx_count - 1, cycle_step, (mixed_in, empty_spec, empty_spec)
    )
    sum_real, sum_imag = add_lag(ctx_count - 1, held_block, sum_real, sum_imag)
    return inverse_tail(sum_real, sum_imag, length)


def per_device(queries, key_input, value_input, filters, skip_gain, out_weight):
    tok_rows, channels = queries.shape
    length = 2 * tok_rows
    mixed_in = (key_input.astype(jnp.float32) * value_input.astype(jnp.float32)).astype(
        jnp.bfloat16
    )
    conv = cycle_conv(mixed_in, filters, length)
    gated = (
        queries.astype(jnp.float32) * (conv + skip_gain[None, :] * mixed_in.astype(jnp.float32))
    ).astype(jnp.bfloat16)
    shares = lax.psum_scatter(
        lax.dot_general(
            out_weight, gated, (((0,), (1,)), ((), ())), preferred_element_type=jnp.float32
        ).astype(jnp.bfloat16),
        "ch",
        scatter_dimension=0,
        tiled=True,
    ).astype(jnp.float32)
    return shares.T.astype(jnp.bfloat16)


def solution(mesh):
    in_specs = (
        P("ctx", "ch"),
        P("ctx", "ch"),
        P("ctx", "ch"),
        P("ctx", "ch"),
        P("ch"),
        P("ch", None),
    )
    out_specs = P("ctx", "ch")
    return jax.shard_map(
        per_device, mesh=mesh, in_specs=in_specs, out_specs=out_specs, check_vma=False
    )
```

profile of v0, /device:TPU:0, one launch (start us, length us, event | category | flops | bytes accessed | tf_op | source)
XLA Modules:
  0.0 963.6 jit_solution(6129385879402401914)
XLA Ops:
  13.3 51.3 %all-gather.2.cloned.1.call-done = bf16[4096,512]{1,0:T(8,128)(2,1)} async-done(((bf16[1024,512]{1,0:T(8,128)(2,1)}), bf16[4096,512]{1,0:T(8,128)(2,1)}) %all-gather.2.cloned.1.call-update) | async-done | bytes 4194320 | tf_op jit(solution)/shard_map/all_gather | solution.py:88
  64.6 4.8 concatenate.3
  69.5 523.9 %while.21 = (s32[]{:T(128)}, bf16[1024,512]{1,0:T(8,128)(2,1)}, f32[64,32,512]{2,1,0:T(8,128)}, f32[64,32,512]{2,1,0:T(8,128)}, bf16[5120,512]{1,0:T(8,128)(2,1)...) while((s32[]{:T(128)}, bf16[1024,512]{1,0:T(8,128)(2,1)}, f32[64,32,512]{2,1,0:T(8,128)}, ...), condition=%wide.region_1.2_spmd.clone, body=%wide.region_0.1_spmd.clone.sunk | while | flops 2483855360 | bytes 476086720 | solution.py:110
  71.2 4.4 collective-permute-start
  80.2 4.9 fusion.855
  87.1 5.2 convolution_add_fusion.6
  98.7 11.0 %subtract_convert_fusion.35 = (bf16[64,32,512]{2,0,1:T(8,128)(2,1)}, bf16[64,32,512]{2,0,1:T(8,128)(2,1)S(1)}, bf16[64,32,512]{2,0,1:T(8,128)(2,1)S(1)}, bf16[64...) fusion(f32[64,32]{0,1:T(8,128)S(1)} %get-tuple-element.274, ...), kind=kOutput, calls=%fused_computation.9.clone.1 | convolution fusion | flops 165748736 | bytes 35667968 | tf_op jit(solution)/shard_map/while/body/eval_jaxpr/kn,nqc->kqc/dot_general | solution.py:28
  128.4 3.8 fusion.862
  139.6 4.1 fusion.856
  151.0 3.8 fusion.860
  154.8 3.8 fusion.871
  169.8 3.8 fusion.868
  177.4 3.9 fusion.858
  181.3 3.8 fusion.873
  185.1 12.3 %add_subtract_fusion.5 = f32[32,64,512]{2,0,1:T(8,128)} fusion(f32[32,64,512]{2,0,1:T(8,128)} %fusion.866, f32[32,64,512]{2,0,1:T(8,128)} %fusion.867, f32[32,64,512]{2,0,1:T(8,128)} %fusion.868, f32[32,64,512]{2,0,1:T(8,128)} %fusion.869, f32[32,64,512]{2,0,1:T(8,128)} %fusion.870, bf16[64,32,512]{2,0,1:T(8,128)(2,1)} %get-tuple-element.277), kind=kOutput, calls=%fused_computation.4.clone.1 | convolution fusion | flops 72367104 | bytes 27262976 | tf_op jit(solution)/shard_map/while/body/eval_jaxpr/kqc,qm->kmc/dot_general | solution.py:28
  197.5 10.7 %add_add_fusion.7 = f32[32,64,512]{2,0,1:T(8,128)} fusion(f32[32,64,512]{2,0,1:T(8,128)S(1)} %copy-done.8, f32[32,64,512]{2,0,1:T(8,128)} %fusion.862, f32[32,64,512]{2,0,1:T(8,128)} %fusion.863, f32[32,64,512]{2,0,1:T(8,128)} %fusion.864, f32[32,64,512]{2,0,1:T(8,128)} %fusion.865, bf16[64,32,512]{2,0,1:T(8,128)(2,1)S(1)} %copy-done.1), kind=kOutput, calls=%fused_computation.12.clone.1 | convolution fusion | flops 72367104 | bytes 27262976 | tf_op jit(solution)/shard_map/while/body/eval_jaxpr/kqc,qm->kmc/dot_general | solution.py:28
  209.7 6.9 add_add_fusion.6
  216.6 17.4 %bitcast_add_fusion.8 = (f32[64,32,512]{2,1,0:T(8,128)}, f32[64,32,512]{2,1,0:T(8,128)}) fusion(f32[64,32,512]{2,1,0:T(8,128)} %get-tuple-element.298, f32[32,64,512]{2,0,1:T(8,128)} %add_add_fusion.6, f32[32,64,512]{2,0,1:T(8,128)} %add_add_fusion.7, f32[32,64,512]{2,0,1:T(8,128)} %add_subtract_fusion.5, pred[]{:T(512)S(6)} %compare.21, ...), kind=kOutput, calls=%fused_computation.clone.1 | convolution fusion | flops 82852864 | bytes 52428800 | tf_op jit(solution)/shard_map/while/body/eval_jaxpr/kqc,qm->kmc/dot_general | solution.py:28
  243.5 4.9 fusion.855
  250.4 5.2 convolution_add_fusion.6
  262.0 21.1 %subtract_convert_fusion.35 = (bf16[64,32,512]{2,0,1:T(8,128)(2,1)}, bf16[64,32,512]{2,0,1:T(8,128)(2,1)S(1)}, bf16[64,32,512]{2,0,1:T(8,128)(2,1)S(1)}, bf16[64...) fusion(f32[64,32]{0,1:T(8,128)S(1)} %get-tuple-element.274, ...), kind=kOutput, calls=%fused_computation.9.clone.1 | convolution fusion | flops 165748736 | bytes 35667968 | tf_op jit(solution)/shard_map/while/body/eval_jaxpr/kn,nqc->kqc/dot_general | solution.py:28
  301.8 3.8 fusion.862
  313.0 4.1 fusion.856
  324.5 3.8 fusion.860
  328.3 3.8 fusion.871
  343.2 3.8 fusion.868
  350.9 3.9 fusion.858
  354.7 3.8 fusion.873
  358.5 12.3 %add_subtract_fusion.5 = f32[32,64,512]{2,0,1:T(8,128)} fusion(f32[32,64,512]{2,0,1:T(8,128)} %fusion.866, f32[32,64,512]{2,0,1:T(8,128)} %fusion.867, f32[32,64,512]{2,0,1:T(8,128)} %fusion.868, f32[32,64,512]{2,0,1:T(8,128)} %fusion.869, f32[32,64,512]{2,0,1:T(8,128)} %fusion.870, bf16[64,32,512]{2,0,1:T(8,128)(2,1)} %get-tuple-element.277), kind=kOutput, calls=%fused_computation.4.clone.1 | convolution fusion | flops 72367104 | bytes 27262976 | tf_op jit(solution)/shard_map/while/body/eval_jaxpr/kqc,qm->kmc/dot_general | solution.py:28
  370.9 10.7 %add_add_fusion.7 = f32[32,64,512]{2,0,1:T(8,128)} fusion(f32[32,64,512]{2,0,1:T(8,128)S(1)} %copy-done.8, f32[32,64,512]{2,0,1:T(8,128)} %fusion.862, f32[32,64,512]{2,0,1:T(8,128)} %fusion.863, f32[32,64,512]{2,0,1:T(8,128)} %fusion.864, f32[32,64,512]{2,0,1:T(8,128)} %fusion.865, bf16[64,32,512]{2,0,1:T(8,128)(2,1)S(1)} %copy-done.1), kind=kOutput, calls=%fused_computation.12.clone.1 | convolution fusion | flops 72367104 | bytes 27262976 | tf_op jit(solution)/shard_map/while/body/eval_jaxpr/kqc,qm->kmc/dot_general | solution.py:28
  383.1 6.9 add_add_fusion.6
  390.0 19.8 %bitcast_add_fusion.8 = (f32[64,32,512]{2,1,0:T(8,128)}, f32[64,32,512]{2,1,0:T(8,128)}) fusion(f32[64,32,512]{2,1,0:T(8,128)} %get-tuple-element.298, f32[32,64,512]{2,0,1:T(8,128)} %add_add_fusion.6, f32[32,64,512]{2,0,1:T(8,128)} %add_add_fusion.7, f32[32,64,512]{2,0,1:T(8,128)} %add_subtract_fusion.5, pred[]{:T(512)S(6)} %compare.21, ...), kind=kOutput, calls=%fused_computation.clone.1 | convolution fusion | flops 82852864 | bytes 52428800 | tf_op jit(solution)/shard_map/while/body/eval_jaxpr/kqc,qm->kmc/dot_general | solution.py:28
  418.4 4.9 fusion.855
  425.4 5.2 convolution_add_fusion.6
  437.0 21.1 %subtract_convert_fusion.35 = (bf16[64,32,512]{2,0,1:T(8,128)(2,1)}, bf16[64,32,512]{2,0,1:T(8,128)(2,1)S(1)}, bf16[64,32,512]{2,0,1:T(8,128)(2,1)S(1)}, bf16[64...) fusion(f32[64,32]{0,1:T(8,128)S(1)} %get-tuple-element.274, ...), kind=kOutput, calls=%fused_computation.9.clone.1 | convolution fusion | flops 165748736 | bytes 35667968 | tf_op jit(solution)/shard_map/while/body/eval_jaxpr/kn,nqc->kqc/dot_general | solution.py:28
  476.8 3.8 fusion.862
  487.9 4.1 fusion.856
  499.4 3.8 fusion.860
  503.2 3.8 fusion.871
  518.2 3.8 fusion.868
  525.8 3.9 fusion.858
  529.7 3.8 fusion.873
  533.5 12.3 %add_subtract_fusion.5 = f32[32,64,512]{2,0,1:T(8,128)} fusion(f32[32,64,512]{2,0,1:T(8,128)} %fusion.866, f32[32,64,512]{2,0,1:T(8,128)} %fusion.867, f32[32,64,512]{2,0,1:T(8,128)} %fusion.868, f32[32,64,512]{2,0,1:T(8,128)} %fusion.869, f32[32,64,512]{2,0,1:T(8,128)} %fusion.870, bf16[64,32,512]{2,0,1:T(8,128)(2,1)} %get-tuple-element.277), kind=kOutput, calls=%fused_computation.4.clone.1 | convolution fusion | flops 72367104 | bytes 27262976 | tf_op jit(solution)/shard_map/while/body/eval_jaxpr/kqc,qm->kmc/dot_general | solution.py:28
  545.9 10.7 %add_add_fusion.7 = f32[32,64,512]{2,0,1:T(8,128)} fusion(f32[32,64,512]{2,0,1:T(8,128)S(1)} %copy-done.8, f32[32,64,512]{2,0,1:T(8,128)} %fusion.862, f32[32,64,512]{2,0,1:T(8,128)} %fusion.863, f32[32,64,512]{2,0,1:T(8,128)} %fusion.864, f32[32,64,512]{2,0,1:T(8,128)} %fusion.865, bf16[64,32,512]{2,0,1:T(8,128)(2,1)S(1)} %copy-done.1), kind=kOutput, calls=%fused_computation.12.clone.1 | convolution fusion | flops 72367104 | bytes 27262976 | tf_op jit(solution)/shard_map/while/body/eval_jaxpr/kqc,qm->kmc/dot_general | solution.py:28
  558.1 6.9 add_add_fusion.6
  564.9 19.8 %bitcast_add_fusion.8 = (f32[64,32,512]{2,1,0:T(8,128)}, f32[64,32,512]{2,1,0:T(8,128)}) fusion(f32[64,32,512]{2,1,0:T(8,128)} %get-tuple-element.298, f32[32,64,512]{2,0,1:T(8,128)} %add_add_fusion.6, f32[32,64,512]{2,0,1:T(8,128)} %add_add_fusion.7, f32[32,64,512]{2,0,1:T(8,128)} %add_subtract_fusion.5, pred[]{:T(512)S(6)} %compare.21, ...), kind=kOutput, calls=%fused_computation.clone.1 | convolution fusion | flops 82852864 | bytes 52428800 | tf_op jit(solution)/shard_map/while/body/eval_jaxpr/kqc,qm->kmc/dot_general | solution.py:28
  601.0 4.9 fusion.328
  605.8 4.5 convolution_add_fusion.3
  610.3 4.5 add_negate_fusion.3
  614.8 5.0 convolution_add_fusion.2
  619.8 11.0 %subtract_convert_fusion.15 = (bf16[64,32,512]{2,0,1:T(8,128)(2,1)}, bf16[64,32,512]{2,0,1:T(8,128)(2,1)S(1)}, bf16[64,32,512]{2,0,1:T(8,128)(2,1)S(1)}, bf16[64...) fusion(f32[64,32]{0,1:T(8,128)S(1)} %copy-done.23, ...), kind=kOutput, calls=%fused_computation.320 | convolution fusion | flops 165748736 | bytes 35667968 | tf_op jit(solution)/shard_map/kn,nqc->kqc/dot_general | solution.py:28
  630.8 3.8 fusion.311
  657.1 3.8 fusion.347
  662.8 3.8 fusion.317
  687.0 3.9 fusion.299
  702.1 9.2 add_subtract_fusion.2
  711.3 11.7 %add_add_fusion.3 = f32[32,64,512]{2,0,1:T(8,128)} fusion(f32[32,64,512]{2,0,1:T(8,128)} %fusion.339, f32[32,64,512]{2,0,1:T(8,128)} %fusion.337, f32[32,64,512]{2,0,1:T(8,128)} %fusion.309, f32[32,64,512]{2,0,1:T(8,128)} %fusion.347, f32[32,64,512]{2,0,1:T(8,128)} %fusion.345, bf16[64,32,512]{2,0,1:T(8,128)(2,1)S(1)} %copy-done.13), kind=kOutput, calls=%fused_computation.323 | convolution fusion | flops 72367104 | bytes 27262976 | tf_op jit(solution)/shard_map/kqc,qm->kmc/dot_general | solution.py:28
  723.0 7.1 add_add_fusion.2
  730.1 19.3 %bitcast_add_fusion.3 = (f32[64,32,512]{2,1,0:T(8,128)}, f32[64,32,512]{2,1,0:T(8,128)}) fusion(f32[64,32,512]{2,1,0:T(8,128)} %get-tuple-element.167, f32[32,64,512]{2,0,1:T(8,128)} %add_add_fusion.2, f32[32,64,512]{2,0,1:T(8,128)} %add_add_fusion.3, f32[32,64,512]{2,0,1:T(8,128)} %add_subtract_fusion.2, f32[64,32,512]{2,1,0:T(8,128)} %get-tuple-element.165, ...), kind=kOutput, calls=%fused_computation.297 | convolution fusion | flops 80755712 | bytes 52428800 | tf_op jit(solution)/shard_map/kqc,qm->kmc/dot_general | solution.py:28
  749.5 6.4 fusion.417
  787.0 59.6 %fusion.356 = (bf16[64,32,512]{2,0,1:T(8,128)(2,1)S(1)}, f32[32,64,512]{2,1,0:T(8,128)}, f32[32,64,512]{2,1,0:T(8,128)}) fusion(f32[64,32]{0,1:T(8,128)S(1)} %copy-done.23, f32[64,32]{0,1:T(8,128)S(1)} %copy-done.24, f32[32,64,512]{2,0,1:T(8,128)} %fusion.417, f32[32,64,512]{2,0,1:T(8,128)} %fusion.502, f32[32,64,512]{2,0,1:T(8,128)} %fusion.419, ...), kind=kLoop, calls=%fused_computation.393 | loop fusion | flops 14680064 | bytes 60833792 | tf_op jit(solution)/shard_map/convert_element_type | solution.py:18
  846.6 3.9 fusion.354
  860.9 6.7 convert_bitcast_fusion
  867.6 88.9 %reduce-scatter.2.cloned.1.call-done = bf16[512,1024]{0,1:T(8,128)(2,1)} async-done(((bf16[4096,1024]{0,1:T(8,128)(2,1)}), bf16[512,1024]{0,1:T(8,128)(2,1)}) %reduce-scatter.2.cloned.1.call-update) | async-done | bytes 1048592 | tf_op jit(solution)/shard_map/reduce_scatter | solution.py:127
  (212 shorter events, 310.1 us)
Async XLA Ops:
  6.5 58.1 %all-gather.2.cloned.1.call-start = ((), (), s32[]{:S(2)}) async-start(), calls=%async_computation.1 | async-start | bytes 5242880 | tf_op jit(solution)/shard_map/all_gather | solution.py:88
  7.3 949.3 %reduce-scatter.2.cloned.1.call-start = ((), (), s32[]{:S(2)}) async-start(), calls=%async_computation.2 | async-start | bytes 9437184 | tf_op jit(solution)/shard_map/reduce_scatter | solution.py:127
  9.2 1.0 copy-start.19
  71.2 162.8 %collective-permute-start = (bf16[1024,512]{1,0:T(8,128)(2,1)S(1)}, bf16[1024,512]{1,0:T(8,128)(2,1)}, u32[]{:S(2)}, u32[]{:S(2)}) collective-permute-start(bf16[1024,512]{1,0:T(8,128)(2,1)S(1)} %copy.397), channel_id=1, source_target_pairs={{0,8},{8,16},{16,24},{1,9},{9,17},{17,25},{2,10},{10,18},{18,26},{... | collective-permute-start | bytes 3145736 | tf_op jit(solution)/shard_map/while/body/eval_jaxpr/ppermute | solution.py:12
  169.8 3.8 copy-start.3
  173.6 3.8 copy-start.2
  177.4 3.9 copy-start
  185.1 12.4 %copy-start.1 = (bf16[64,32,512]{2,0,1:T(8,128)(2,1)S(1)}, bf16[64,32,512]{2,0,1:T(8,128)(2,1)}, u32[]{:S(2)}) copy-start(bf16[64,32,512]{2,0,1:T(8,128)(2,1)} %get-tuple-element.283) | copy-start | bytes 6291460 | tf_op jit(solution)/shard_map/while
  185.1 12.4 %copy-start.8 = (f32[32,64,512]{2,0,1:T(8,128)S(1)}, f32[32,64,512]{2,0,1:T(8,128)}, u32[]{:S(2)}) copy-start(f32[32,64,512]{2,0,1:T(8,128)} %fusion.861) | copy-start | bytes 12582916 | tf_op jit(solution)/shard_map/while
  197.5 10.7 %copy-start.4 = (f32[32,64,512]{2,0,1:T(8,128)S(1)}, f32[32,64,512]{2,0,1:T(8,128)}, u32[]{:S(2)}) copy-start(f32[32,64,512]{2,0,1:T(8,128)} %fusion.856) | copy-start | bytes 12582916 | tf_op jit(solution)/shard_map/while
  197.5 10.7 %copy-start.5 = (f32[32,64,512]{2,0,1:T(8,128)S(1)}, f32[32,64,512]{2,0,1:T(8,128)}, u32[]{:S(2)}) copy-start(f32[32,64,512]{2,0,1:T(8,128)} %fusion.857) | copy-start | bytes 12582916 | tf_op jit(solution)/shard_map/while
  197.5 10.7 %copy-start.6 = (f32[32,64,512]{2,0,1:T(8,128)S(1)}, f32[32,64,512]{2,0,1:T(8,128)}, u32[]{:S(2)}) copy-start(f32[32,64,512]{2,0,1:T(8,128)} %fusion.859) | copy-start | bytes 12582916 | tf_op jit(solution)/shard_map/while
  197.5 12.2 %copy-start.7 = (f32[32,64,512]{2,0,1:T(8,128)S(1)}, f32[32,64,512]{2,0,1:T(8,128)}, u32[]{:S(2)}) copy-start(f32[32,64,512]{2,0,1:T(8,128)} %fusion.860) | copy-start | bytes 12582916 | tf_op jit(solution)/shard_map/while
  235.5 174.3 %collective-permute-start = (bf16[1024,512]{1,0:T(8,128)(2,1)S(1)}, bf16[1024,512]{1,0:T(8,128)(2,1)}, u32[]{:S(2)}, u32[]{:S(2)}) collective-permute-start(bf16[1024,512]{1,0:T(8,128)(2,1)S(1)} %copy.397), channel_id=1, source_target_pairs={{0,8},{8,16},{16,24},{1,9},{9,17},{17,25},{2,10},{10,18},{18,26},{... | collective-permute-start | bytes 3145736 | tf_op jit(solution)/shard_map/while/body/eval_jaxpr/ppermute | solution.py:12
  343.2 3.8 copy-start.3
  347.1 3.8 copy-start.2
  350.9 3.9 copy-start
  358.5 12.4 %copy-start.1 = (bf16[64,32,512]{2,0,1:T(8,128)(2,1)S(1)}, bf16[64,32,512]{2,0,1:T(8,128)(2,1)}, u32[]{:S(2)}) copy-start(bf16[64,32,512]{2,0,1:T(8,128)(2,1)} %get-tuple-element.283) | copy-start | bytes 6291460 | tf_op jit(solution)/shard_map/while
  358.5 12.4 %copy-start.8 = (f32[32,64,512]{2,0,1:T(8,128)S(1)}, f32[32,64,512]{2,0,1:T(8,128)}, u32[]{:S(2)}) copy-start(f32[32,64,512]{2,0,1:T(8,128)} %fusion.861) | copy-start | bytes 12582916 | tf_op jit(solution)/shard_map/while
  370.9 10.7 %copy-start.4 = (f32[32,64,512]{2,0,1:T(8,128)S(1)}, f32[32,64,512]{2,0,1:T(8,128)}, u32[]{:S(2)}) copy-start(f32[32,64,512]{2,0,1:T(8,128)} %fusion.856) | copy-start | bytes 12582916 | tf_op jit(solution)/shard_map/while
  370.9 10.7 %copy-start.5 = (f32[32,64,512]{2,0,1:T(8,128)S(1)}, f32[32,64,512]{2,0,1:T(8,128)}, u32[]{:S(2)}) copy-start(f32[32,64,512]{2,0,1:T(8,128)} %fusion.857) | copy-start | bytes 12582916 | tf_op jit(solution)/shard_map/while
  370.9 10.7 %copy-start.6 = (f32[32,64,512]{2,0,1:T(8,128)S(1)}, f32[32,64,512]{2,0,1:T(8,128)}, u32[]{:S(2)}) copy-start(f32[32,64,512]{2,0,1:T(8,128)} %fusion.859) | copy-start | bytes 12582916 | tf_op jit(solution)/shard_map/while
  370.9 12.2 %copy-start.7 = (f32[32,64,512]{2,0,1:T(8,128)S(1)}, f32[32,64,512]{2,0,1:T(8,128)}, u32[]{:S(2)}) copy-start(f32[32,64,512]{2,0,1:T(8,128)} %fusion.860) | copy-start | bytes 12582916 | tf_op jit(solution)/shard_map/while
  411.4 173.4 %collective-permute-start = (bf16[1024,512]{1,0:T(8,128)(2,1)S(1)}, bf16[1024,512]{1,0:T(8,128)(2,1)}, u32[]{:S(2)}, u32[]{:S(2)}) collective-permute-start(bf16[1024,512]{1,0:T(8,128)(2,1)S(1)} %copy.397), channel_id=1, source_target_pairs={{0,8},{8,16},{16,24},{1,9},{9,17},{17,25},{2,10},{10,18},{18,26},{... | collective-permute-start | bytes 3145736 | tf_op jit(solution)/shard_map/while/body/eval_jaxpr/ppermute | solution.py:12
  518.2 3.8 copy-start.3
  522.0 3.8 copy-start.2
  525.8 3.9 copy-start
  533.5 12.4 %copy-start.1 = (bf16[64,32,512]{2,0,1:T(8,128)(2,1)S(1)}, bf16[64,32,512]{2,0,1:T(8,128)(2,1)}, u32[]{:S(2)}) copy-start(bf16[64,32,512]{2,0,1:T(8,128)(2,1)} %get-tuple-element.283) | copy-start | bytes 6291460 | tf_op jit(solution)/shard_map/while
  533.5 12.4 %copy-start.8 = (f32[32,64,512]{2,0,1:T(8,128)S(1)}, f32[32,64,512]{2,0,1:T(8,128)}, u32[]{:S(2)}) copy-start(f32[32,64,512]{2,0,1:T(8,128)} %fusion.861) | copy-start | bytes 12582916 | tf_op jit(solution)/shard_map/while
  545.8 10.7 %copy-start.4 = (f32[32,64,512]{2,0,1:T(8,128)S(1)}, f32[32,64,512]{2,0,1:T(8,128)}, u32[]{:S(2)}) copy-start(f32[32,64,512]{2,0,1:T(8,128)} %fusion.856) | copy-start | bytes 12582916 | tf_op jit(solution)/shard_map/while
  545.8 10.7 %copy-start.5 = (f32[32,64,512]{2,0,1:T(8,128)S(1)}, f32[32,64,512]{2,0,1:T(8,128)}, u32[]{:S(2)}) copy-start(f32[32,64,512]{2,0,1:T(8,128)} %fusion.857) | copy-start | bytes 12582916 | tf_op jit(solution)/shard_map/while
  545.9 10.7 %copy-start.6 = (f32[32,64,512]{2,0,1:T(8,128)S(1)}, f32[32,64,512]{2,0,1:T(8,128)}, u32[]{:S(2)}) copy-start(f32[32,64,512]{2,0,1:T(8,128)} %fusion.859) | copy-start | bytes 12582916 | tf_op jit(solution)/shard_map/while
  545.9 12.2 %copy-start.7 = (f32[32,64,512]{2,0,1:T(8,128)S(1)}, f32[32,64,512]{2,0,1:T(8,128)}, u32[]{:S(2)}) copy-start(f32[32,64,512]{2,0,1:T(8,128)} %fusion.860) | copy-start | bytes 12582916 | tf_op jit(solution)/shard_map/while
  593.4 4.6 copy-start.21
  614.8 5.0 copy-start.23
  614.8 5.0 copy-start.24
  690.9 3.7 copy-start.14
  694.6 3.7 copy-start.13
  694.6 7.5 copy-start.18
  698.4 3.7 copy-start.17
  711.3 11.7 %copy-start.15 = (f32[32,64,512]{2,0,1:T(8,128)S(1)}, f32[32,64,512]{2,0,1:T(8,128)}, u32[]{:S(2)}) copy-start(f32[32,64,512]{2,0,1:T(8,128)} %fusion.317) | copy-start | bytes 12582916
  711.3 11.7 %copy-start.16 = (f32[32,64,512]{2,0,1:T(8,128)S(1)}, f32[32,64,512]{2,0,1:T(8,128)}, u32[]{:S(2)}) copy-start(f32[32,64,512]{2,0,1:T(8,128)} %fusion.325) | copy-start | bytes 12582916
  749.4 6.4 copy-start.10
  755.9 3.4 copy-start.9
  846.6 3.9 copy-start.25
  850.5 2.2 copy-start.11
  850.5 3.5 copy-start.12
  850.5 3.5 copy-start.26
  858.0 1.3 copy-start.20
  858.0 1.5 copy-start.22
  858.0 1.5 copy-start.27
  858.1 2.8 copy-start.28
Sparse Core Ops, SparseCore 0:
  9.2 55.3 all-gather.1
  867.8 88.6 reduce-scatter.1
where the time goes:
time: 966 us; the launch traced here: 964 us
  matrix products  694 us (72%)
  waiting for transfers between devices  141 us (15%)
  other arithmetic  68.2 us (7%)
  local copies, waits for them, and re-layouts  26 us (3%)
  between operations  13.9 us (1%)
  starting transfers between devices  10.3 us (1%)
  loops' own time  10 us (1%)
    dot_general x146, matrix products, split_dot(): jnp.einsum(form, left_piece, right_piece, preferred_element_type=jnp.floa...  688 us
    reduce_scatter x1, waiting for transfers between devices, per_device(): lax.psum_scatter(lax.dot_general(out_weight, gated, (((0,), (1,)), ((), (...  88.9 us
    convert_element_type x2, other arithmetic, split_pieces(): high_part = values.astype(jnp.bfloat16)  63.5 us
    all_gather x1, waiting for transfers between devices, cycle_conv(): all_segments = lax.all_gather(filters, 'ctx', axis=0, tiled=True)  51.3 us
  transfers between devices with their start and end apart: 5, of which 2 were waited for; matrix products, arithmetic and copies ran while one was open for 52% of the time, Pallas kernels for 0%

commit v1 on v0

v1 whole, which is shorter than its diff:
```python
import functools
import math

import jax
import jax.numpy as jnp
import numpy as np
from jax import lax
from jax.experimental import pallas as pl
from jax.experimental.pallas import tpu as pltpu
from jax.sharding import PartitionSpec as P

BLOCK = 256
F32 = jnp.float32
BF16 = jnp.bfloat16


def transform_tables(block):
    k = np.arange(block)[:, None]
    n = np.arange(block)[None, :]
    angle = np.pi * (((2 * k + 1) * n) % (4 * block)) / (2 * block)
    forward = np.concatenate([np.cos(angle), -np.sin(angle)], axis=0)
    backward = np.concatenate([np.cos(angle).T, -np.sin(angle).T], axis=1) / block

    def halves(table):
        high = table.astype(BF16)
        low = (table - high.astype(np.float64)).astype(BF16)
        return high, low

    f_high, f_low = halves(forward)
    b_high, b_low = halves(backward)
    return np.stack([f_high, f_low]), np.stack([b_high, b_low])


def dot(left, right):
    return jnp.dot(left, right, preferred_element_type=F32)


def conv_kernel(pair_ref, f_ref, b_ref, out_ref, spec, prod):
    nb, block, width2 = pair_ref.shape
    width = width2 // 2

    def ahead(p, carry):
        data = pair_ref[p]
        spec[p] = dot(f_ref[0], data) + dot(f_ref[1], data)
        return carry

    lax.fori_loop(0, nb, ahead, 0)

    rows = 8
    sign = 1.0 - 2.0 * (lax.broadcasted_iota(jnp.int32, (rows, width), 0) % 2).astype(F32)

    def products(chunk, carry):
        top = pl.multiple_of(chunk * rows, rows)
        re = pl.ds(top, rows)
        im = pl.ds(pl.multiple_of(block + top, rows), rows)
        x = [(spec[p, re, :width], spec[p, im, :width]) for p in range(nb)]
        h = [(spec[p, re, width:], spec[p, im, width:]) for p in range(nb)]
        last = None
        for j in range(nb):
            zr = zi = None
            for p in range(j + 1):
                xr, xi = x[p]
                hr, hi = h[j - p]
                tr = xr * hr - xi * hi
                ti = xr * hi + xi * hr
                zr = tr if zr is None else zr + tr
                zi = ti if zi is None else zi + ti
            if last is None:
                yr, yi = zr, zi
            else:
                yr = zr - sign * last[1]
                yi = zi + sign * last[0]
            last = (zr, zi)
            prod[j, re, :] = yr
            prod[j, im, :] = yi
        return carry

    lax.fori_loop(0, block // rows, products, 0)

    def back(j, carry):
        data = jnp.concatenate([prod[2 * j], prod[2 * j + 1]], axis=1)
        high = data.astype(BF16)
        low = (data - high.astype(F32)).astype(BF16)
        conv = (dot(b_ref[0], high) + (dot(b_ref[0], low) + dot(b_ref[1], high))).astype(BF16)
        out_ref[2 * j] = conv[:, :width]
        out_ref[2 * j + 1] = conv[:, width:]
        return carry

    lax.fori_loop(0, nb // 2, back, 0)


def causal_conv(pair):
    total, width2 = pair.shape
    width = width2 // 2
    nb = total // BLOCK
    forward, backward = transform_tables(BLOCK)
    out = pl.pallas_call(
        conv_kernel,
        out_shape=jax.ShapeDtypeStruct((nb, BLOCK, width), BF16),
        in_specs=[pl.BlockSpec(memory_space=pltpu.VMEM)] * 3,
        out_specs=pl.BlockSpec(memory_space=pltpu.VMEM),
        scratch_shapes=[
            pltpu.VMEM((nb, 2 * BLOCK, width2), F32),
            pltpu.VMEM((nb, 2 * BLOCK, width), F32),
        ],
        compiler_params=pltpu.CompilerParams(vmem_limit_bytes=48 * 1024 * 1024),
        cost_estimate=pl.CostEstimate(
            flops=14 * total * BLOCK * width2, bytes_accessed=6 * total * width, transcendentals=0
        ),
    )(pair.reshape(nb, BLOCK, width2), jnp.asarray(forward), jnp.asarray(backward))
    return out.reshape(total, width)


def per_device(queries, key_input, value_input, filters, skip_gain, out_weight):
    tok_rows, channels = queries.shape
    n_ctx = lax.axis_size("ctx")
    width = channels // n_ctx
    mixed_in = (key_input.astype(F32) * value_input.astype(F32)).astype(BF16)
    split = lambda a: a.reshape(tok_rows, n_ctx, width)
    pair = jnp.concatenate([split(mixed_in), split(filters)], axis=2).transpose(1, 0, 2)
    pair = lax.all_to_all(pair, "ctx", 0, 0, tiled=True)
    conv = causal_conv(pair.reshape(n_ctx * tok_rows, 2 * width))
    conv = lax.all_to_all(conv.reshape(n_ctx, tok_rows, width), "ctx", 0, 0, tiled=True)
    conv = conv.transpose(1, 0, 2).reshape(tok_rows, channels).astype(F32)
    gated = (
        queries.astype(F32) * (conv + skip_gain[None, :] * mixed_in.astype(F32))
    ).astype(BF16)
    shares = lax.psum_scatter(
        lax.dot_general(
            out_weight, gated, (((0,), (1,)), ((), ())), preferred_element_type=F32
        ).astype(BF16),
        "ch",
        scatter_dimension=0,
        tiled=True,
    ).astype(F32)
    return shares.T.astype(BF16)


def solution(mesh):
    in_specs = (
        P("ctx", "ch"),
        P("ctx", "ch"),
        P("ctx", "ch"),
        P("ctx", "ch"),
        P("ch"),
        P("ch", None),
    )
    return jax.shard_map(
        per_device, mesh=mesh, in_specs=in_specs, out_specs=P("ctx", "ch"), check_vma=False
    )
```

time: 966 us -> 172 us (0.18)
  matrix products: 694 us -> 6.9 us
  other arithmetic: 68.2 us -> 2.12 us
  waiting for transfers between devices: 141 us -> 89.5 us
  blocking collectives: 0 us -> 45.8 us
  local copies, waits for them, and re-layouts: 26 us -> 1.26 us
  Pallas kernels: 0 us -> 13 us
  starting transfers between devices: 10.3 us -> 0.01 us
  loops' own time: 10 us -> 0 us
    dot_general x146 -> x0, matrix products: 688 us -> none  [split_dot(): jnp.einsum(form, left_piece, right_piece, preferred_element_type=jnp.floa...]
    convert_element_type x4 -> x0, other arithmetic: 65.8 us -> none  [the longest x2 63.5 us: split_pieces(): high_part = values.astype(jnp.bfloat16)]
    all_gather x1 -> x0, waiting for transfers between devices: 51.3 us -> none  [cycle_conv(): all_segments = lax.all_gather(filters, 'ctx', axis=0, tiled=True)]
    all_to_all x0 -> x2, blocking collectives: none -> 45.8 us  [the longest x1 30.5 us: per_device(): pair = lax.all_to_all(pair, 'ctx', 0, 0, tiled=True)]
    pallas_call x0 -> x1, Pallas kernels: none -> 13 us  [causal_conv(): pl.pallas_call(conv_kernel, out_shape=jax.ShapeDtypeStruct((nb, BLOCK, wi...]
    ppermute x3 -> x0, starting transfers between devices: 10.3 us -> none  [shifted(): return lax.ppermute(block, axis, route)]
    another operation x1 -> x0, loops' own time: 10 us -> none  [cycle_conv(): lax.fori_loop(0, ctx_count - 1, cycle_step, (mixed_in, empty_spec, empty_...]
  transfers between devices with their start and end apart: 5 -> 1, of which waited for: 2 -> 1; matrix products, arithmetic and copies ran while one was open for 52% -> 0% of each run, Pallas kernels for 0% -> 0%
where the time goes in v1:
time: 172 us
  waiting for transfers between devices  89.5 us (52%)
  blocking collectives  45.8 us (27%)
  between operations  13.5 us (8%)
  Pallas kernels  13 us (8%)
  matrix products  6.9 us (4%)
  other arithmetic  2.12 us (1%)
    reduce_scatter x1, waiting for transfers between devices, per_device(): lax.psum_scatter(lax.dot_general(out_weight, gated, (((0,), (1,)), ((), (...  89.5 us
    all_to_all x1, blocking collectives, per_device(): pair = lax.all_to_all(pair, 'ctx', 0, 0, tiled=True)  30.5 us
    all_to_all x1, blocking collectives, per_device(): lax.all_to_all(conv.reshape(n_ctx, tok_rows, width), 'ctx', 0, 0, tiled=T...  15.4 us
    pallas_call x1, Pallas kernels, causal_conv(): pl.pallas_call(conv_kernel, out_shape=jax.ShapeDtypeStruct((nb, BLOCK, wi...  13 us
    dot_general x1, matrix products, per_device(): lax.dot_general(out_weight, gated, (((0,), (1,)), ((), ())), preferred_el...  6.9 us
  transfers between devices with their start and end apart: 1, of which 1 were waited for; matrix products, arithmetic and copies ran while one was open for 0% of the time, Pallas kernels for 0%

profile of v1, /device:TPU:0, one launch (start us, length us, event | category | flops | bytes accessed | tf_op | source)
XLA Modules:
  0.0 172.1 jit_solution(1531241254369850357)
XLA Ops:
  6.5 0.0 copy-start
  6.5 0.0 reduce-scatter.2.cloned.1.call-start
  6.5 1.2 copy-done
  7.8 1.9 %copy_bitcast_fusion = (bf16[1024,4,128]{2,0,1:T(8,128)(2,1)S(1)}, bf16[1024,4,128]{2,0,1:T(8,128)(2,1)S(1)}) fusion(bf16[1024,512]{1,0:T(8,128)(2,1)} %param.10, bf16[1024,512]{1,0:T(8,128)(2,1)} %param.9, bf16[1024,512]{1,0:T(8,128)(2,1)S(1)} %copy-done), kind=kLoop, calls=%fused_computation.7 | loop fusion | flops 2097152 | bytes 5242880 | tf_op jit(solution)/shard_map/reshape | solution.py:119
  9.7 0.2 maximum_bitcast_fusion
  9.9 0.0 copy-start.1
  9.9 0.0 copy-start.2
  9.9 30.5 %all_to_all.10 = bf16[4,1024,256]{2,1,0:T(8,128)(2,1)S(1)} all-to-all(bf16[4,1024,256]{2,1,0:T(8,128)(2,1)S(1)} %maximum_bitcast_fusion), channel_id=1, replica_groups=mesh['ctx'=4,'ch'=8] {'ctx'}, dimensions={0} | all-to-all | bytes 4194304 | tf_op jit(solution)/shard_map/all_to_all | solution.py:121
  40.4 0.0 copy-done.1
  40.4 0.0 copy-done.2
  40.4 0.0 copy-start.5
  40.4 0.0 copy-start.6
  40.4 0.0 copy-start.7
  40.4 13.0 %shard_map.82 = bf16[16,256,128]{2,1,0:T(8,128)(2,1)S(1)} custom-call(bf16[16,256,256]{2,1,0:T(8,128)(2,1)S(1)} %bitcast.30, bf16[2,512,256]{2,1,0:T(8,128)(2,1)S(1)} %copy-done.2, bf16[2,256,512]{2,1,0:T(8,128)(2,1)S(1)} %copy-done.1), custom_call_target="tpu_custom_call" | custom-call | flops 3758096384 | bytes 3145728 | tf_op jit(solution)/shard_map/pallas_call | solution.py:97
  53.4 0.0 copy-start.3
  53.4 0.0 copy-start.4
  53.5 15.4 %all_to_all.11 = bf16[4,1024,128]{2,1,0:T(8,128)(2,1)S(1)} all-to-all(bf16[4,1024,128]{2,1,0:T(8,128)(2,1)S(1)} %bitcast.31), channel_id=1, replica_groups=mesh['ctx'=4,'ch'=8] {'ctx'}, dimensions={0} | all-to-all | bytes 2097152 | tf_op jit(solution)/shard_map/all_to_all | solution.py:123
  68.8 0.0 copy-done.5
  68.8 0.0 copy-done.6
  68.8 0.0 copy-done.7
  68.8 0.0 copy-done.3
  68.8 0.0 copy-done.4
  68.9 6.9 %convert_bitcast_fusion = bf16[4096,1024]{0,1:T(8,128)(2,1)} fusion(bf16[512,4096]{1,0:T(8,128)(2,1)S(1)} %copy-done.5, bf16[1024,512]{1,0:T(8,128)(2,1)S(1)} %copy-done.6, f32[512]{0:T(512)S(1)} %copy-done.7, bf16[1024,512]{1,0:T(8,128)(2,1)S(1)} %copy-done.3, bf16[1024,512]{1,0:T(8,128)(2,1)S(1)} %copy-done.4, bf16[4,1024,128]{2,1,0:T(8,128)(2,1)S(1)} %all_to_all.11), kind=kOutput, calls=%fused_computation | convolution fusion | flops 4304928768 | bytes 16779264 | tf_op jit(solution)/shard_map/dot_general | solution.py:129
  75.7 0.0 reduce-scatter.2.cloned.1.call-update
  75.8 89.5 %reduce-scatter.2.cloned.1.call-done = bf16[512,1024]{0,1:T(8,128)(2,1)} async-done(((bf16[4096,1024]{0,1:T(8,128)(2,1)}), bf16[512,1024]{0,1:T(8,128)(2,1)}) %reduce-scatter.2.cloned.1.call-update) | async-done | bytes 1048592 | tf_op jit(solution)/shard_map/reduce_scatter | solution.py:128
Async XLA Ops:
  6.5 1.2 copy-start
  6.5 158.7 %reduce-scatter.2.cloned.1.call-start = ((), (), s32[]{:S(2)}) async-start(), calls=%async_computation.3 | async-start | bytes 9437184 | tf_op jit(solution)/shard_map/reduce_scatter | solution.py:128
  9.9 30.5 %copy-start.1 = (bf16[2,256,512]{2,1,0:T(8,128)(2,1)S(1)}, bf16[2,256,512]{2,1,0:T(8,128)(2,1)}, u32[]{:S(2)}) copy-start(bf16[2,256,512]{2,1,0:T(8,128)(2,1)} %constant.5.clone.b_ref) | copy-start | bytes 1572868
  9.9 30.5 %copy-start.2 = (bf16[2,512,256]{2,1,0:T(8,128)(2,1)S(1)}, bf16[2,512,256]{2,1,0:T(8,128)(2,1)}, u32[]{:S(2)}) copy-start(bf16[2,512,256]{2,1,0:T(8,128)(2,1)} %constant.4.clone.f_ref) | copy-start | bytes 1572868
  40.4 28.4 %copy-start.5 = (bf16[512,4096]{1,0:T(8,128)(2,1)S(1)}, bf16[512,4096]{1,0:T(8,128)(2,1)}, u32[]{:S(2)}) copy-start(bf16[512,4096]{1,0:T(8,128)(2,1)} %param.13) | copy-start | bytes 12582916
  40.4 28.4 %copy-start.6 = (bf16[1024,512]{1,0:T(8,128)(2,1)S(1)}, bf16[1024,512]{1,0:T(8,128)(2,1)}, u32[]{:S(2)}) copy-start(bf16[1024,512]{1,0:T(8,128)(2,1)} %param.8) | copy-start | bytes 3145732
  40.4 28.4 %copy-start.7 = (f32[512]{0:T(512)S(1)}, f32[512]{0:T(512)}, u32[]{:S(2)}) copy-start(f32[512]{0:T(512)} %param.12) | copy-start | bytes 6148
  53.4 15.4 %copy-start.3 = (bf16[1024,512]{1,0:T(8,128)(2,1)S(1)}, bf16[1024,512]{1,0:T(8,128)(2,1)}, u32[]{:S(2)}) copy-start(bf16[1024,512]{1,0:T(8,128)(2,1)} %param.10) | copy-start | bytes 3145732
  53.4 15.4 %copy-start.4 = (bf16[1024,512]{1,0:T(8,128)(2,1)S(1)}, bf16[1024,512]{1,0:T(8,128)(2,1)}, u32[]{:S(2)}) copy-start(bf16[1024,512]{1,0:T(8,128)(2,1)} %param.9) | copy-start | bytes 3145732
Sparse Core Ops, SparseCore 0:
  75.9 89.3 reduce-scatter.1

commit v2 on v1

--- a/solution.py
+++ b/solution.py
@@ -1,5 +1,4 @@
 import functools
-import math
 
 import jax
 import jax.numpy as jnp
@@ -111,6 +110,191 @@
     return out.reshape(total, width)
 
 
+MESH = pl.DeviceIdType.MESH
+CHUNKS = 8
+
+
+def project_kernel(n_ch, g_ref, w_ref, out_ref, wx, gx, send, from_left, from_right, own,
+                   w_send, w_recv, g_send, g_recv, send_sem, left_sem, right_sem):
+    me = lax.axis_index("ch")
+    chip = lax.div(me, 2)
+    core = lax.rem(me, 2)
+    mate = chip * 2 + 1 - core
+    n_chip = n_ch // 2
+    tokens, block = out_ref.shape
+    rows = tokens // CHUNKS
+    has_left = chip > 0
+    has_right = chip < n_chip - 1
+    left = jnp.maximum(me - 2, core)
+    right = jnp.minimum(me + 2, n_ch - 2 + core)
+
+    barrier = pltpu.get_barrier_semaphore()
+    pl.semaphore_signal(barrier, inc=1, device_id={"ch": mate}, device_id_type=MESH)
+
+    @pl.when(has_left)
+    def _():
+        pl.semaphore_signal(barrier, inc=1, device_id={"ch": left}, device_id_type=MESH)
+
+    @pl.when(has_right)
+    def _():
+        pl.semaphore_signal(barrier, inc=1, device_id={"ch": right}, device_id_type=MESH)
+
+    pl.semaphore_wait(barrier, 1 + has_left.astype(jnp.int32) + has_right.astype(jnp.int32))
+
+    def columns(chip_at, core_at):
+        return pl.ds(pl.multiple_of((chip_at * 2 + core_at) * block, block), block)
+
+    def tokens_of(m):
+        return pl.ds(pl.multiple_of(m * rows, rows), rows)
+
+    def remote(src, dst, sent, arrived, target):
+        return pltpu.make_async_remote_copy(
+            src_ref=src, dst_ref=dst, send_sem=sent, recv_sem=arrived,
+            device_id={"ch": target}, device_id_type=MESH,
+        )
+
+    def g_copy(m):
+        at = tokens_of(m)
+        return remote(g_ref.at[at], gx.at[at], g_send.at[m], g_recv.at[m], mate)
+
+    def w_copy(t):
+        return remote(w_ref.at[:, columns(t, 1 - core)], wx.at[t], w_send.at[t], w_recv.at[t], mate)
+
+    def to_right(t, m):
+        at = tokens_of(m)
+        return remote(send.at[t, at], from_left.at[t, at], send_sem.at[t, m], left_sem.at[t, m], right)
+
+    def to_left(t, m):
+        at = tokens_of(m)
+        return remote(send.at[t, at], from_right.at[t, at], send_sem.at[t, m], right_sem.at[t, m], left)
+
+    def arrive_left(t, m):
+        at = tokens_of(m)
+        return remote(send.at[t, at], from_left.at[t, at], send_sem.at[t, m], left_sem.at[t, m], left)
+
+    def arrive_right(t, m):
+        at = tokens_of(m)
+        return remote(send.at[t, at], from_right.at[t, at], send_sem.at[t, m], right_sem.at[t, m], right)
+
+    for t in range(n_chip):
+        w_copy(t).start()
+    for m in range(CHUNKS):
+        g_copy(m).start()
+    for t in range(n_chip):
+        w_copy(t).wait()
+
+    def share(t, m):
+        at = tokens_of(m)
+        return dot(g_ref[at, :], w_ref[:, columns(t, core)]) + dot(gx[at, :], wx[t])
+
+    def pass_on(t, m, first, arrived, copy):
+        at = tokens_of(m)
+        part = share(t, m)
+
+        @pl.when(first)
+        def _():
+            send[t, at, :] = part.astype(BF16)
+
+        @pl.when(jnp.logical_not(first))
+        def _():
+            arrived(t, m)
+
+        @pl.when(jnp.logical_not(first))
+        def _():
+            buffer = from_left if copy is to_right else from_right
+            send[t, at, :] = (part + buffer[t, at, :].astype(F32)).astype(BF16)
+
+        copy(t, m).start()
+
+    def drain(m):
+        for d in range(n_chip - 1, 0, -1):
+            @pl.when(chip + d < n_chip)
+            def _():
+                to_right(chip + d, m).wait_send()
+
+            @pl.when(chip - d >= 0)
+            def _():
+                to_left(chip - d, m).wait_send()
+
+    def step(m, carry):
+        g_copy(m).wait()
+
+        @pl.when(m >= 2)
+        def _():
+            drain(m - 2)
+
+        for d in range(n_chip - 1, 0, -1):
+            @pl.when(chip + d < n_chip)
+            def _():
+                pass_on(chip + d, m, jnp.logical_not(has_left),
+                        lambda t, m: arrive_left(t, m).wait_recv(), to_right)
+
+            @pl.when(chip - d >= 0)
+            def _():
+                pass_on(chip - d, m, jnp.logical_not(has_right),
+                        lambda t, m: arrive_right(t, m).wait_recv(), to_left)
+
+        own[tokens_of(m), :] = share(chip, m)
+        return carry
+
+    lax.fori_loop(0, CHUNKS, step, 0)
+
+    def finish(m, carry):
+        at = tokens_of(m)
+
+        @pl.when(has_left)
+        def _():
+            arrive_left(chip, m).wait_recv()
+            own[at, :] += from_left[chip, at, :].astype(F32)
+
+        @pl.when(has_right)
+        def _():
+            arrive_right(chip, m).wait_recv()
+            own[at, :] += from_right[chip, at, :].astype(F32)
+
+        out_ref[at, :] = own[at, :].astype(BF16)
+        return carry
+
+    lax.fori_loop(0, CHUNKS, finish, 0)
+    drain(CHUNKS - 2)
+    drain(CHUNKS - 1)
+
+
+def project(gated, out_weight):
+    tokens, channels = gated.shape
+    n_ch = lax.axis_size("ch")
+    n_chip = n_ch // 2
+    block = out_weight.shape[1] // n_ch
+    return pl.pallas_call(
+        functools.partial(project_kernel, n_ch),
+        out_shape=jax.ShapeDtypeStruct((tokens, block), BF16),
+        in_specs=[pl.BlockSpec(memory_space=pltpu.VMEM)] * 2,
+        out_specs=pl.BlockSpec(memory_space=pltpu.VMEM),
+        scratch_shapes=[
+            pltpu.VMEM((n_chip, channels, block), BF16),
+            pltpu.VMEM((tokens, channels), BF16),
+            pltpu.VMEM((n_chip, tokens, block), BF16),
+            pltpu.VMEM((n_chip, tokens, block), BF16),
+            pltpu.VMEM((n_chip, tokens, block), BF16),
+            pltpu.VMEM((tokens, block), F32),
+            pltpu.SemaphoreType.DMA((n_chip,)),
+            pltpu.SemaphoreType.DMA((n_chip,)),
+            pltpu.SemaphoreType.DMA((CHUNKS,)),
+            pltpu.SemaphoreType.DMA((CHUNKS,)),
+            pltpu.SemaphoreType.DMA((n_chip, CHUNKS)),
+            pltpu.SemaphoreType.DMA((n_chip, CHUNKS)),
+            pltpu.SemaphoreType.DMA((n_chip, CHUNKS)),
+        ],
+        compiler_params=pltpu.CompilerParams(
+            collective_id=0, has_side_effects=True, vmem_limit_bytes=48 * 1024 * 1024
+        ),
+        cost_estimate=pl.CostEstimate(
+            flops=2 * tokens * channels * n_ch * block,
+            bytes_accessed=2 * channels * n_ch * block, transcendentals=0,
+        ),
+    )(gated, out_weight)
+
+
 def per_device(queries, key_input, value_input, filters, skip_gain, out_weight):
     tok_rows, channels = queries.shape
     n_ctx = lax.axis_size("ctx")
@@ -125,15 +309,7 @@
     gated = (
         queries.astype(F32) * (conv + skip_gain[None, :] * mixed_in.astype(F32))
     ).astype(BF16)
-    shares = lax.psum_scatter(
-        lax.dot_general(
-            out_weight, gated, (((0,), (1,)), ((), ())), preferred_element_type=F32
-        ).astype(BF16),
-        "ch",
-        scatter_dimension=0,
-        tiled=True,
-    ).astype(F32)
-    return shares.T.astype(BF16)
+    return project(gated, out_weight)
 
 
 def solution(mesh):

time: 172 us -> 152 us (0.88)
  waiting for transfers between devices: 89.5 us -> 0 us
  Pallas kernels: 13 us -> 95.5 us
  between operations: 13.5 us -> 0.05 us
  matrix products: 6.9 us -> 0 us
  local copies, waits for them, and re-layouts: 1.26 us -> 6.24 us
  other arithmetic: 2.12 us -> 4.07 us
    reduce_scatter x1 -> x0, waiting for transfers between devices: 89.5 us -> none  [per_device(): lax.psum_scatter(lax.dot_general(out_weight, gated, (((0,), (1,)), ((), (...]
    pallas_call x0 -> x1, Pallas kernels: none -> 82.5 us  [project(): pl.pallas_call(functools.partial(project_kernel, n_ch), out_shape=jax.Sha...]
    dot_general x1 -> x0, matrix products: 6.9 us -> none  [per_device(): lax.dot_general(out_weight, gated, (((0,), (1,)), ((), ())), preferred_el...]
    transpose x0 -> x1, local copies, waits for them, and re-layouts: none -> 2.62 us  [per_device(): jnp.concatenate([split(mixed_in), split(filters)], axis=2)]
    convert_element_type x0 -> x2, other arithmetic: none -> 2.36 us  [the longest x1 1.91 us: per_device(): mixed_in = (key_input.astype(F32) * value_input.astype(F32)).astype(BF16)]
    reshape x1 -> x0, other arithmetic: 1.89 us -> none  [per_device(): split = lambda a: a.reshape(tok_rows, n_ctx, width)]
  transfers between devices with their start and end apart: 1 -> 0, of which waited for: 1 -> 0; matrix products, arithmetic and copies ran while one was open for 0% -> 0% of each run, Pallas kernels for 0% -> 0%
where the time goes in v2:
time: 152 us
  Pallas kernels  95.5 us (63%)
  blocking collectives  46 us (30%)
  local copies, waits for them, and re-layouts  6.24 us (4%)
  other arithmetic  4.07 us (3%)
    pallas_call x1, Pallas kernels, project(): pl.pallas_call(functools.partial(project_kernel, n_ch), out_shape=jax.Sha...  82.5 us
    all_to_all x1, blocking collectives, per_device(): pair = lax.all_to_all(pair, 'ctx', 0, 0, tiled=True)  30.7 us
    all_to_all x1, blocking collectives, per_device(): lax.all_to_all(conv.reshape(n_ctx, tok_rows, width), 'ctx', 0, 0, tiled=T...  15.4 us
    pallas_call x1, Pallas kernels, causal_conv(): pl.pallas_call(conv_kernel, out_shape=jax.ShapeDtypeStruct((nb, BLOCK, wi...  13 us

profile of v2, /device:TPU:0, one launch (start us, length us, event | category | flops | bytes accessed | tf_op | source)
XLA Modules:
  0.0 151.9 jit_solution(14939972706699139092)
XLA Ops:
  0.0 0.0 copy-start.2
  0.0 1.9 %multiply_convert_fusion = bf16[1024,512]{1,0:T(8,128)(2,1)S(1)} fusion(bf16[1024,512]{1,0:T(8,128)(2,1)} %param.10, bf16[1024,512]{1,0:T(8,128)(2,1)} %param.9), kind=kLoop, calls=%fused_computation.5 | loop fusion | flops 2097152 | bytes 3145728 | tf_op jit(solution)/shard_map/convert_element_type | solution.py:302
  1.9 1.3 copy.17
  3.2 0.0 copy-done.2
  3.2 1.3 copy.13
  4.5 1.7 %maximum_bitcast_fusion = bf16[4,1024,256]{1,2,0:T(8,128)(2,1)S(1)} fusion(bf16[1024,4,128]{0,2,1:T(8,128)(2,1)} %bitcast.19, bf16[1024,4,128]{0,2,1:T(8,128)(2,1)} %bitcast.18), kind=kLoop, calls=%fused_computation.3 | loop fusion | flops 4194304 | bytes 4194304 | tf_op jit(solution)/shard_map/transpose | solution.py:304
  6.3 2.6 %copy.15 = bf16[4,1024,256]{2,1,0:T(8,128)(2,1)} copy(bf16[4,1024,256]{1,2,0:T(8,128)(2,1)S(1)} %maximum_bitcast_fusion) | data formatting | bytes 4194304 | tf_op jit(solution)/shard_map/transpose | solution.py:304
  8.9 0.0 copy-start
  8.9 0.0 copy-start.1
  8.9 30.7 %all_to_all.10 = bf16[4,1024,256]{2,1,0:T(8,128)(2,1)S(1)} all-to-all(bf16[4,1024,256]{2,1,0:T(8,128)(2,1)} %copy.15), channel_id=1, replica_groups=mesh['ctx'=4,'ch'=8] {'ctx'}, dimensions={0} | all-to-all | bytes 4194304 | tf_op jit(solution)/shard_map/all_to_all | solution.py:305
  39.6 0.0 copy-done
  39.6 0.0 copy-done.1
  39.6 13.0 %shard_map.82 = bf16[16,256,128]{2,1,0:T(8,128)(2,1)S(1)} custom-call(bf16[16,256,256]{2,1,0:T(8,128)(2,1)S(1)} %bitcast.16, bf16[2,512,256]{2,1,0:T(8,128)(2,1)S(1)} %copy-done.1, bf16[2,256,512]{2,1,0:T(8,128)(2,1)S(1)} %copy-done), custom_call_target="tpu_custom_call" | custom-call | flops 3758096384 | bytes 3145728 | tf_op jit(solution)/shard_map/pallas_call | solution.py:96
  52.6 0.0 copy-start.3
  52.6 0.0 copy-start.4
  52.6 15.4 %all_to_all.11 = bf16[4,1024,128]{2,1,0:T(8,128)(2,1)S(1)} all-to-all(bf16[4,1024,128]{2,1,0:T(8,128)(2,1)S(1)} %bitcast.17), channel_id=1, replica_groups=mesh['ctx'=4,'ch'=8] {'ctx'}, dimensions={0} | all-to-all | bytes 2097152 | tf_op jit(solution)/shard_map/all_to_all | solution.py:307
  68.0 0.0 copy-done.3
  68.0 0.0 copy-done.4
  68.0 0.4 fusion.1.g_ref
  68.4 82.5 %shard_map.83 = bf16[1024,512]{1,0:T(8,128)(2,1)S(1)} custom-call(bf16[1024,512]{1,0:T(8,128)(2,1)S(1)} %fusion.1.g_ref, bf16[512,4096]{1,0:T(8,128)(2,1)} %w_ref.1), custom_call_target="tpu_custom_call" | custom-call | flops 4294967296 | bytes 4194304 | tf_op jit(solution)/shard_map/pallas_call | solution.py:268
  150.9 1.0 copy.21
Async XLA Ops:
  0.0 3.2 %copy-start.2 = (bf16[1024,512]{1,0:T(8,128)(2,1)S(1)}, bf16[1024,512]{1,0:T(8,128)(2,1)}, u32[]{:S(2)}) copy-start(bf16[1024,512]{1,0:T(8,128)(2,1)} %param.11) | copy-start | bytes 3145732
  8.9 30.7 %copy-start = (bf16[2,256,512]{2,1,0:T(8,128)(2,1)S(1)}, bf16[2,256,512]{2,1,0:T(8,128)(2,1)}, u32[]{:S(2)}) copy-start(bf16[2,256,512]{2,1,0:T(8,128)(2,1)} %constant.5.clone.b_ref) | copy-start | bytes 1572868
  8.9 30.7 %copy-start.1 = (bf16[2,512,256]{2,1,0:T(8,128)(2,1)S(1)}, bf16[2,512,256]{2,1,0:T(8,128)(2,1)}, u32[]{:S(2)}) copy-start(bf16[2,512,256]{2,1,0:T(8,128)(2,1)} %constant.4.clone.f_ref) | copy-start | bytes 1572868
  52.6 15.4 %copy-start.3 = (bf16[1024,512]{1,0:T(8,128)(2,1)S(1)}, bf16[1024,512]{1,0:T(8,128)(2,1)}, u32[]{:S(2)}) copy-start(bf16[1024,512]{1,0:T(8,128)(2,1)} %param.8) | copy-start | bytes 3145732
  52.6 15.4 %copy-start.4 = (f32[512]{0:T(512)S(1)}, f32[512]{0:T(512)}, u32[]{:S(2)}) copy-start(f32[512]{0:T(512)} %param.12) | copy-start | bytes 6148

commit v3 on v2

--- a/solution.py
+++ b/solution.py
@@ -34,16 +34,102 @@
     return jnp.dot(left, right, preferred_element_type=F32)
 
 
-def conv_kernel(pair_ref, f_ref, b_ref, out_ref, spec, prod):
-    nb, block, width2 = pair_ref.shape
-    width = width2 // 2
-
-    def ahead(p, carry):
-        data = pair_ref[p]
-        spec[p] = dot(f_ref[0], data) + dot(f_ref[1], data)
+MESH = pl.DeviceIdType.MESH
+
+
+def gate_kernel(n_ctx, q_ref, k_ref, v_ref, h_ref, skip_ref, f_ref, b_ref, w_ref, out_ref, wx,
+                outbox, inbox, spec, prod, conv_out, conv_in,
+                w_send, w_recv, in_send, in_recv, back_send, back_recv):
+    me = lax.axis_index("ctx")
+    ch = lax.axis_index("ch")
+    core = lax.rem(ch, 2)
+    mate = ch + 1 - 2 * core
+    n_chip, _, wide = wx.shape
+    tokens = q_ref.shape[0]
+    width = conv_in.shape[2]
+    block = BLOCK
+    per = tokens // block
+    nb = n_ctx * per
+
+    barrier = pltpu.get_barrier_semaphore()
+    pl.semaphore_signal(barrier, inc=1, device_id={"ch": mate}, device_id_type=MESH)
+    for d in range(1, n_ctx):
+        pl.semaphore_signal(
+            barrier, inc=1, device_id={"ctx": lax.rem(me + d, n_ctx)}, device_id_type=MESH
+        )
+
+    def rows_of(r):
+        return pl.ds(pl.multiple_of(r * block, block), block)
+
+    def fill(r, carry):
+        at = rows_of(r)
+        for i in range(n_ctx):
+            lanes = slice(i * width, (i + 1) * width)
+            mixed = k_ref[at, lanes].astype(F32) * v_ref[at, lanes].astype(F32)
+            outbox[i, at, :width] = mixed.astype(BF16)
+            outbox[i, at, width:] = h_ref[at, lanes]
         return carry
 
-    lax.fori_loop(0, nb, ahead, 0)
+    lax.fori_loop(0, per, fill, 0)
+    pl.semaphore_wait(barrier, n_ctx)
+
+    def in_copy(d):
+        to = lax.rem(me + d, n_ctx)
+        return pltpu.make_async_remote_copy(
+            src_ref=outbox.at[to], dst_ref=inbox.at[me],
+            send_sem=in_send.at[d], recv_sem=in_recv.at[d],
+            device_id={"ctx": to}, device_id_type=MESH,
+        )
+
+    def in_wait(d):
+        source = lax.rem(me + n_ctx - d, n_ctx)
+        pltpu.make_async_remote_copy(
+            src_ref=outbox.at[source], dst_ref=inbox.at[source],
+            send_sem=in_send.at[d], recv_sem=in_recv.at[d],
+            device_id={"ctx": source}, device_id_type=MESH,
+        ).wait_recv()
+
+    def back_copy(d):
+        to = lax.rem(me + d, n_ctx)
+        return pltpu.make_async_remote_copy(
+            src_ref=conv_out.at[to], dst_ref=conv_in.at[me],
+            send_sem=back_send.at[d], recv_sem=back_recv.at[d],
+            device_id={"ctx": to}, device_id_type=MESH,
+        )
+
+    def back_wait(d):
+        source = lax.rem(me + n_ctx - d, n_ctx)
+        pltpu.make_async_remote_copy(
+            src_ref=conv_out.at[source], dst_ref=conv_in.at[source],
+            send_sem=back_send.at[d], recv_sem=back_recv.at[d],
+            device_id={"ctx": source}, device_id_type=MESH,
+        ).wait_recv()
+
+    def w_copy(t):
+        lanes = pl.ds(pl.multiple_of((t * 2 + 1 - core) * wide, wide), wide)
+        return pltpu.make_async_remote_copy(
+            src_ref=w_ref.at[:, lanes], dst_ref=wx.at[t],
+            send_sem=w_send.at[t], recv_sem=w_recv.at[t],
+            device_id={"ch": mate}, device_id_type=MESH,
+        )
+
+    for d in range(1, n_ctx):
+        in_copy(d).start()
+    for t in range(n_chip):
+        w_copy(t).start()
+
+    def ahead(box, source):
+        def one(r, carry):
+            data = box[source, rows_of(r), :]
+            spec[source * per + r] = dot(f_ref[0], data) + dot(f_ref[1], data)
+            return carry
+
+        lax.fori_loop(0, per, one, 0)
+
+    ahead(outbox, me)
+    for d in range(1, n_ctx):
+        in_wait(d)
+        ahead(inbox, lax.rem(me + n_ctx - d, n_ctx))
 
     rows = 8
     sign = 1.0 - 2.0 * (lax.broadcasted_iota(jnp.int32, (rows, width), 0) % 2).astype(F32)
@@ -76,46 +162,91 @@
 
     lax.fori_loop(0, block // rows, products, 0)
 
-    def back(j, carry):
-        data = jnp.concatenate([prod[2 * j], prod[2 * j + 1]], axis=1)
-        high = data.astype(BF16)
-        low = (data - high.astype(F32)).astype(BF16)
-        conv = (dot(b_ref[0], high) + (dot(b_ref[0], low) + dot(b_ref[1], high))).astype(BF16)
-        out_ref[2 * j] = conv[:, :width]
-        out_ref[2 * j + 1] = conv[:, width:]
+    def back(box, to):
+        def one(r, carry):
+            j = to * per + 2 * r
+            data = jnp.concatenate([prod[j], prod[j + 1]], axis=1)
+            high = data.astype(BF16)
+            low = (data - high.astype(F32)).astype(BF16)
+            conv = (dot(b_ref[0], high) + (dot(b_ref[0], low) + dot(b_ref[1], high))).astype(BF16)
+            box[to, rows_of(2 * r), :] = conv[:, :width]
+            box[to, rows_of(2 * r + 1), :] = conv[:, width:]
+            return carry
+
+        lax.fori_loop(0, per // 2, one, 0)
+
+    for d in range(1, n_ctx):
+        back(conv_out, lax.rem(me + d, n_ctx))
+        back_copy(d).start()
+    back(conv_in, me)
+    for d in range(1, n_ctx):
+        back_wait(d)
+
+    def gate(r, carry):
+        at = rows_of(r)
+        for i in range(n_ctx):
+            lanes = slice(i * width, (i + 1) * width)
+            mixed = outbox[i, at, :width].astype(F32)
+            total = conv_in[i, at, :].astype(F32) + skip_ref[:, lanes] * mixed
+            out_ref[at, lanes] = (q_ref[at, lanes].astype(F32) * total).astype(BF16)
         return carry
 
-    lax.fori_loop(0, nb // 2, back, 0)
-
-
-def causal_conv(pair):
-    total, width2 = pair.shape
-    width = width2 // 2
-    nb = total // BLOCK
+    lax.fori_loop(0, per, gate, 0)
+    for d in range(1, n_ctx):
+        in_copy(d).wait_send()
+        back_copy(d).wait_send()
+    for t in range(n_chip):
+        w_copy(t).wait()
+
+
+def gated_conv(queries, key_input, value_input, filters, skip_gain, out_weight):
+    tokens, channels = queries.shape
+    n_ctx = lax.axis_size("ctx")
+    n_ch = lax.axis_size("ch")
+    n_chip = n_ch // 2
+    width = channels // n_ctx
+    nb = n_ctx * tokens // BLOCK
     forward, backward = transform_tables(BLOCK)
-    out = pl.pallas_call(
-        conv_kernel,
-        out_shape=jax.ShapeDtypeStruct((nb, BLOCK, width), BF16),
-        in_specs=[pl.BlockSpec(memory_space=pltpu.VMEM)] * 3,
-        out_specs=pl.BlockSpec(memory_space=pltpu.VMEM),
+    vmem = pl.BlockSpec(memory_space=pltpu.VMEM)
+    hbm = pl.BlockSpec(memory_space=pl.ANY)
+    return pl.pallas_call(
+        functools.partial(gate_kernel, n_ctx),
+        out_shape=(
+            jax.ShapeDtypeStruct((tokens, channels), BF16),
+            jax.ShapeDtypeStruct((n_chip, channels, out_weight.shape[1] // n_ch), BF16),
+        ),
+        in_specs=[vmem] * 7 + [hbm],
+        out_specs=(vmem, hbm),
         scratch_shapes=[
-            pltpu.VMEM((nb, 2 * BLOCK, width2), F32),
+            pltpu.VMEM((n_ctx, tokens, 2 * width), BF16),
+            pltpu.VMEM((n_ctx, tokens, 2 * width), BF16),
+            pltpu.VMEM((nb, 2 * BLOCK, 2 * width), F32),
             pltpu.VMEM((nb, 2 * BLOCK, width), F32),
+            pltpu.VMEM((n_ctx, tokens, width), BF16),
+            pltpu.VMEM((n_ctx, tokens, width), BF16),
+            pltpu.SemaphoreType.DMA((n_chip,)),
+            pltpu.SemaphoreType.DMA((n_chip,)),
+            pltpu.SemaphoreType.DMA((n_ctx,)),
+            pltpu.SemaphoreType.DMA((n_ctx,)),
+            pltpu.SemaphoreType.DMA((n_ctx,)),
+            pltpu.SemaphoreType.DMA((n_ctx,)),
         ],
-        compiler_params=pltpu.CompilerParams(vmem_limit_bytes=48 * 1024 * 1024),
+        compiler_params=pltpu.CompilerParams(
+            collective_id=1, has_side_effects=True, vmem_limit_bytes=56 * 1024 * 1024
+        ),
         cost_estimate=pl.CostEstimate(
-            flops=14 * total * BLOCK * width2, bytes_accessed=6 * total * width, transcendentals=0
+            flops=28 * n_ctx * tokens * BLOCK * width, bytes_accessed=10 * tokens * channels,
+            transcendentals=0,
         ),
-    )(pair.reshape(nb, BLOCK, width2), jnp.asarray(forward), jnp.asarray(backward))
-    return out.reshape(total, width)
-
-
-MESH = pl.DeviceIdType.MESH
+    )(queries, key_input, value_input, filters, skip_gain[None, :],
+      jnp.asarray(forward), jnp.asarray(backward), out_weight)
+
+
 CHUNKS = 8
 
 
-def project_kernel(n_ch, g_ref, w_ref, out_ref, wx, gx, send, from_left, from_right, own,
-                   w_send, w_recv, g_send, g_recv, send_sem, left_sem, right_sem):
+def project_kernel(n_ch, g_ref, w_ref, wx, out_ref, gx, send, from_left, from_right, own,
+                   g_send, g_recv, send_sem, left_sem, right_sem):
     me = lax.axis_index("ch")
     chip = lax.div(me, 2)
     core = lax.rem(me, 2)
@@ -157,9 +288,6 @@
         at = tokens_of(m)
         return remote(g_ref.at[at], gx.at[at], g_send.at[m], g_recv.at[m], mate)
 
-    def w_copy(t):
-        return remote(w_ref.at[:, columns(t, 1 - core)], wx.at[t], w_send.at[t], w_recv.at[t], mate)
-
     def to_right(t, m):
         at = tokens_of(m)
         return remote(send.at[t, at], from_left.at[t, at], send_sem.at[t, m], left_sem.at[t, m], right)
@@ -176,12 +304,8 @@
         at = tokens_of(m)
         return remote(send.at[t, at], from_right.at[t, at], send_sem.at[t, m], right_sem.at[t, m], right)
 
-    for t in range(n_chip):
-        w_copy(t).start()
     for m in range(CHUNKS):
         g_copy(m).start()
-    for t in range(n_chip):
-        w_copy(t).wait()
 
     def share(t, m):
         at = tokens_of(m)
@@ -260,7 +384,7 @@
     drain(CHUNKS - 1)
 
 
-def project(gated, out_weight):
+def project(gated, out_weight, mate_weight):
     tokens, channels = gated.shape
     n_ch = lax.axis_size("ch")
     n_chip = n_ch // 2
@@ -268,17 +392,14 @@
     return pl.pallas_call(
         functools.partial(project_kernel, n_ch),
         out_shape=jax.ShapeDtypeStruct((tokens, block), BF16),
-        in_specs=[pl.BlockSpec(memory_space=pltpu.VMEM)] * 2,
+        in_specs=[pl.BlockSpec(memory_space=pltpu.VMEM)] * 3,
         out_specs=pl.BlockSpec(memory_space=pltpu.VMEM),
         scratch_shapes=[
-            pltpu.VMEM((n_chip, channels, block), BF16),
             pltpu.VMEM((tokens, channels), BF16),
             pltpu.VMEM((n_chip, tokens, block), BF16),
             pltpu.VMEM((n_chip, tokens, block), BF16),
             pltpu.VMEM((n_chip, tokens, block), BF16),
             pltpu.VMEM((tokens, block), F32),
-            pltpu.SemaphoreType.DMA((n_chip,)),
-            pltpu.SemaphoreType.DMA((n_chip,)),
             pltpu.SemaphoreType.DMA((CHUNKS,)),
             pltpu.SemaphoreType.DMA((CHUNKS,)),
             pltpu.SemaphoreType.DMA((n_chip, CHUNKS)),
@@ -292,24 +413,14 @@
             flops=2 * tokens * channels * n_ch * block,
             bytes_accessed=2 * channels * n_ch * block, transcendentals=0,
         ),
-    )(gated, out_weight)
+    )(gated, out_weight, mate_weight)
 
 
 def per_device(queries, key_input, value_input, filters, skip_gain, out_weight):
-    tok_rows, channels = queries.shape
-    n_ctx = lax.axis_size("ctx")
-    width = channels // n_ctx
-    mixed_in = (key_input.astype(F32) * value_input.astype(F32)).astype(BF16)
-    split = lambda a: a.reshape(tok_rows, n_ctx, width)
-    pair = jnp.concatenate([split(mixed_in), split(filters)], axis=2).transpose(1, 0, 2)
-    pair = lax.all_to_all(pair, "ctx", 0, 0, tiled=True)
-    conv = causal_conv(pair.reshape(n_ctx * tok_rows, 2 * width))
-    conv = lax.all_to_all(conv.reshape(n_ctx, tok_rows, width), "ctx", 0, 0, tiled=True)
-    conv = conv.transpose(1, 0, 2).reshape(tok_rows, channels).astype(F32)
-    gated = (
-        queries.astype(F32) * (conv + skip_gain[None, :] * mixed_in.astype(F32))
-    ).astype(BF16)
-    return project(gated, out_weight)
+    gated, mate_weight = gated_conv(
+        queries, key_input, value_input, filters, skip_gain, out_weight
+    )
+    return project(gated, out_weight, mate_weight)
 
 
 def solution(mesh):

time: 152 us -> 135 us (0.89)
  blocking collectives: 46 us -> 0 us
  Pallas kernels: 95.5 us -> 131 us
  other arithmetic: 4.07 us -> 0 us
  local copies, waits for them, and re-layouts: 6.24 us -> 3.78 us
    all_to_all x2 -> x0, blocking collectives: 46 us -> none  [the longest x1 30.7 us: per_device(): pair = lax.all_to_all(pair, 'ctx', 0, 0, tiled=True)]
    pallas_call x1, Pallas kernels: 13 us -> 52.2 us  [gated_conv(): pl.pallas_call(functools.partial(gate_kernel, n_ctx), out_shape=(jax.Shap...]
    pallas_call x1, Pallas kernels: 82.5 us -> 79.2 us  [project(): pl.pallas_call(functools.partial(project_kernel, n_ch), out_shape=jax.Sha...]
    transpose x1 -> x0, local copies, waits for them, and re-layouts: 2.62 us -> none  [per_device(): jnp.concatenate([split(mixed_in), split(filters)], axis=2)]
    convert_element_type x2 -> x0, other arithmetic: 2.36 us -> none  [the longest x1 1.91 us: per_device(): mixed_in = (key_input.astype(F32) * value_input.astype(F32)).astype(BF16)]
    transpose x1 -> x0, other arithmetic: 1.71 us -> none  [per_device(): jnp.concatenate([split(mixed_in), split(filters)], axis=2)]
    unnamed x12 -> x5, local copies, waits for them, and re-layouts: 2.3 us -> 3.78 us
where the time goes in v3:
time: 135 us
  Pallas kernels  131 us (97%)
  local copies, waits for them, and re-layouts  3.78 us (3%)
    pallas_call x1, Pallas kernels, project(): pl.pallas_call(functools.partial(project_kernel, n_ch), out_shape=jax.Sha...  79.2 us
    pallas_call x1, Pallas kernels, gated_conv(): pl.pallas_call(functools.partial(gate_kernel, n_ctx), out_shape=(jax.Shap...  52.2 us
    unnamed x5, local copies, waits for them, and re-layouts  3.78 us

profile of v3, /device:TPU:0, one launch (start us, length us, event | category | flops | bytes accessed | tf_op | source)
XLA Modules:
  0.0 135.2 jit_solution(15055982057985394088)
XLA Ops:
  0.0 52.2 %shard_map.82 = (bf16[1024,512]{1,0:T(8,128)(2,1)}, bf16[4,512,512]{2,1,0:T(8,128)(2,1)}) custom-call(bf16[1024,512]{1,0:T(8,128)(2,1)} %q_ref.1, bf16[1024,512]{1,0:T(8,128)(2,1)} %k_ref.1, bf16[1024,512]{1,0:T(8,128)(2,1)} %v_ref.1, bf16[1024,512]{1,0:T(8,128)(2,1)} %h_ref.1, f32[1,512]{1,0:T(1,128)} %bitcast.1, bf16[2,512,256]{2,1,0:T(8,128)(2,1)} %constant.4.clone.f_ref, ...), custom_call_target="tpu_custom_call" | custom-call | flops 3758096384 | bytes 5242880 | tf_op jit(solution)/shard_map/pallas_call | solution.py:212
  52.2 0.0 copy-start
  52.2 1.6 %copy-done = bf16[4,512,512]{2,1,0:T(8,128)(2,1)S(1)} copy-done((bf16[4,512,512]{2,1,0:T(8,128)(2,1)S(1)}, bf16[4,512,512]{2,1,0:T(8,128)(2,1)}, u32[]{:S(2)}) %copy-start) | copy-done | bytes 2097176
  53.8 0.0 copy-start.1
  53.8 1.2 copy-done.1
  55.0 79.2 %shard_map.83 = bf16[1024,512]{1,0:T(8,128)(2,1)S(1)} custom-call(bf16[1024,512]{1,0:T(8,128)(2,1)S(1)} %copy-done.1, bf16[512,4096]{1,0:T(8,128)(2,1)} %w_ref.3, bf16[4,512,512]{2,1,0:T(8,128)(2,1)S(1)} %copy-done), custom_call_target="tpu_custom_call" | custom-call | flops 4294967296 | bytes 4194304 | tf_op jit(solution)/shard_map/pallas_call | solution.py:392
  134.2 1.0 copy.10
Async XLA Ops:
  52.2 1.6 %copy-start = (bf16[4,512,512]{2,1,0:T(8,128)(2,1)S(1)}, bf16[4,512,512]{2,1,0:T(8,128)(2,1)}, u32[]{:S(2)}) copy-start(bf16[4,512,512]{2,1,0:T(8,128)(2,1)} %get-tuple-element.8.wx) | copy-start | bytes 6291460
  53.8 1.2 copy-start.1

commit v4 on v3

--- a/solution.py
+++ b/solution.py
@@ -242,7 +242,7 @@
       jnp.asarray(forward), jnp.asarray(backward), out_weight)
 
 
-CHUNKS = 8
+CHUNKS = 4
 
 
 def project_kernel(n_ch, g_ref, w_ref, wx, out_ref, gx, send, from_left, from_right, own,

time: 135 us -> 135 us (level)
  no operation moved by 1% of the time
where the time goes in v4:
time: 135 us
  Pallas kernels  131 us (97%)
  local copies, waits for them, and re-layouts  3.78 us (3%)
    pallas_call x1, Pallas kernels, project(): pl.pallas_call(functools.partial(project_kernel, n_ch), out_shape=jax.Sha...  78.7 us
    pallas_call x1, Pallas kernels, gated_conv(): pl.pallas_call(functools.partial(gate_kernel, n_ctx), out_shape=(jax.Shap...  52.2 us
    unnamed x5, local copies, waits for them, and re-layouts  3.78 us

profile of v4, /device:TPU:0, one launch (start us, length us, event | category | flops | bytes accessed | tf_op | source)
XLA Modules:
  0.0 134.7 jit_solution(11039700997035867272)
XLA Ops:
  0.0 52.2 %shard_map.82 = (bf16[1024,512]{1,0:T(8,128)(2,1)}, bf16[4,512,512]{2,1,0:T(8,128)(2,1)}) custom-call(bf16[1024,512]{1,0:T(8,128)(2,1)} %q_ref.1, bf16[1024,512]{1,0:T(8,128)(2,1)} %k_ref.1, bf16[1024,512]{1,0:T(8,128)(2,1)} %v_ref.1, bf16[1024,512]{1,0:T(8,128)(2,1)} %h_ref.1, f32[1,512]{1,0:T(1,128)} %bitcast.1, bf16[2,512,256]{2,1,0:T(8,128)(2,1)} %constant.4.clone.f_ref, ...), custom_call_target="tpu_custom_call" | custom-call | flops 3758096384 | bytes 5242880 | tf_op jit(solution)/shard_map/pallas_call | solution.py:212
  52.2 0.0 copy-start
  52.2 1.6 %copy-done = bf16[4,512,512]{2,1,0:T(8,128)(2,1)S(1)} copy-done((bf16[4,512,512]{2,1,0:T(8,128)(2,1)S(1)}, bf16[4,512,512]{2,1,0:T(8,128)(2,1)}, u32[]{:S(2)}) %copy-start) | copy-done | bytes 2097176
  53.8 0.0 copy-start.1
  53.8 1.2 copy-done.1
  55.0 78.7 %shard_map.83 = bf16[1024,512]{1,0:T(8,128)(2,1)S(1)} custom-call(bf16[1024,512]{1,0:T(8,128)(2,1)S(1)} %copy-done.1, bf16[512,4096]{1,0:T(8,128)(2,1)} %w_ref.3, bf16[4,512,512]{2,1,0:T(8,128)(2,1)S(1)} %copy-done), custom_call_target="tpu_custom_call" | custom-call | flops 4294967296 | bytes 4194304 | tf_op jit(solution)/shard_map/pallas_call | solution.py:392
  133.7 1.0 copy.10
Async XLA Ops:
  52.2 1.6 %copy-start = (bf16[4,512,512]{2,1,0:T(8,128)(2,1)S(1)}, bf16[4,512,512]{2,1,0:T(8,128)(2,1)}, u32[]{:S(2)}) copy-start(bf16[4,512,512]{2,1,0:T(8,128)(2,1)} %get-tuple-element.8.wx) | copy-start | bytes 6291460
  53.8 1.2 copy-start.1

commit v5 on v4

--- a/solution.py
+++ b/solution.py
@@ -245,7 +245,7 @@
 CHUNKS = 4
 
 
-def project_kernel(n_ch, g_ref, w_ref, wx, out_ref, gx, send, from_left, from_right, own,
+def project_kernel(n_ch, g_ref, w_ref, wx, out_ref, w_own, w_sem, gx, send, from_left, from_right, own,
                    g_send, g_recv, send_sem, left_sem, right_sem):
     me = lax.axis_index("ch")
     chip = lax.div(me, 2)
@@ -259,6 +259,13 @@
     left = jnp.maximum(me - 2, core)
     right = jnp.minimum(me + 2, n_ch - 2 + core)
 
+    def w_load(t):
+        lanes = pl.ds(pl.multiple_of((t * 2 + core) * block, block), block)
+        return pltpu.make_async_copy(w_ref.at[:, lanes], w_own.at[t], w_sem.at[t])
+
+    for t in range(n_chip):
+        w_load(t).start()
+
     barrier = pltpu.get_barrier_semaphore()
     pl.semaphore_signal(barrier, inc=1, device_id={"ch": mate}, device_id_type=MESH)
 
@@ -307,9 +314,12 @@
     for m in range(CHUNKS):
         g_copy(m).start()
 
+    for t in range(n_chip):
+        w_load(t).wait()
+
     def share(t, m):
         at = tokens_of(m)
-        return dot(g_ref[at, :], w_ref[:, columns(t, core)]) + dot(gx[at, :], wx[t])
+        return dot(g_ref[at, :], w_own[t]) + dot(gx[at, :], wx[t])
 
     def pass_on(t, m, first, arrived, copy):
         at = tokens_of(m)
@@ -392,9 +402,15 @@
     return pl.pallas_call(
         functools.partial(project_kernel, n_ch),
         out_shape=jax.ShapeDtypeStruct((tokens, block), BF16),
-        in_specs=[pl.BlockSpec(memory_space=pltpu.VMEM)] * 3,
+        in_specs=[
+            pl.BlockSpec(memory_space=pltpu.VMEM),
+            pl.BlockSpec(memory_space=pl.ANY),
+            pl.BlockSpec(memory_space=pltpu.VMEM),
+        ],
         out_specs=pl.BlockSpec(memory_space=pltpu.VMEM),
         scratch_shapes=[
+            pltpu.VMEM((n_chip, channels, block), BF16),
+            pltpu.SemaphoreType.DMA((n_chip,)),
             pltpu.VMEM((tokens, channels), BF16),
             pltpu.VMEM((n_chip, tokens, block), BF16),
             pltpu.VMEM((n_chip, tokens, block), BF16),

time: 135 us -> 133 us (0.985)
  Pallas kernels: 131 us -> 129 us
    pallas_call x1, Pallas kernels: 78.7 us -> 76.5 us  [project(): pl.pallas_call(functools.partial(project_kernel, n_ch), out_shape=jax.Sha...]
where the time goes in v5:
time: 133 us
  Pallas kernels  129 us (97%)
  local copies, waits for them, and re-layouts  3.78 us (3%)
    pallas_call x1, Pallas kernels, project(): pl.pallas_call(functools.partial(project_kernel, n_ch), out_shape=jax.Sha...  76.5 us
    pallas_call x1, Pallas kernels, gated_conv(): pl.pallas_call(functools.partial(gate_kernel, n_ctx), out_shape=(jax.Shap...  52.2 us
    unnamed x5, local copies, waits for them, and re-layouts  3.78 us

profile of v5, /device:TPU:0, one launch (start us, length us, event | category | flops | bytes accessed | tf_op | source)
XLA Modules:
  0.0 132.5 jit_solution(11921819182328567715)
XLA Ops:
  0.0 52.2 %shard_map.82 = (bf16[1024,512]{1,0:T(8,128)(2,1)}, bf16[4,512,512]{2,1,0:T(8,128)(2,1)}) custom-call(bf16[1024,512]{1,0:T(8,128)(2,1)} %q_ref.1, bf16[1024,512]{1,0:T(8,128)(2,1)} %k_ref.1, bf16[1024,512]{1,0:T(8,128)(2,1)} %v_ref.1, bf16[1024,512]{1,0:T(8,128)(2,1)} %h_ref.1, f32[1,512]{1,0:T(1,128)} %bitcast.1, bf16[2,512,256]{2,1,0:T(8,128)(2,1)} %constant.4.clone.f_ref, ...), custom_call_target="tpu_custom_call" | custom-call | flops 3758096384 | bytes 5242880 | tf_op jit(solution)/shard_map/pallas_call | solution.py:212
  52.2 0.0 copy-start
  52.2 1.6 %copy-done = bf16[4,512,512]{2,1,0:T(8,128)(2,1)S(1)} copy-done((bf16[4,512,512]{2,1,0:T(8,128)(2,1)S(1)}, bf16[4,512,512]{2,1,0:T(8,128)(2,1)}, u32[]{:S(2)}) %copy-start) | copy-done | bytes 2097176
  53.8 0.0 copy-start.1
  53.8 1.2 copy-done.1
  55.0 76.5 %shard_map.83 = bf16[1024,512]{1,0:T(8,128)(2,1)S(1)} custom-call(bf16[1024,512]{1,0:T(8,128)(2,1)S(1)} %copy-done.1, bf16[512,4096]{1,0:T(8,128)(2,1)} %w_ref.3, bf16[4,512,512]{2,1,0:T(8,128)(2,1)S(1)} %copy-done), custom_call_target="tpu_custom_call" | custom-call | flops 4294967296 | bytes 4194304 | tf_op jit(solution)/shard_map/pallas_call | solution.py:402
  131.5 1.0 copy.10
Async XLA Ops:
  52.2 1.6 %copy-start = (bf16[4,512,512]{2,1,0:T(8,128)(2,1)S(1)}, bf16[4,512,512]{2,1,0:T(8,128)(2,1)}, u32[]{:S(2)}) copy-start(bf16[4,512,512]{2,1,0:T(8,128)(2,1)} %get-tuple-element.8.wx) | copy-start | bytes 6291460
  53.8 1.2 copy-start.1
